TPU v7x, 512 devices: a whole 4x4x16 slice. The times are simulated.
512 devices in a mesh: lat: 16 (over y, z_hi, core), head: 32 (over z_lo, x).
Axes of the slice: x: 4, y: 4, z: 16 (z_hi: 2, z_lo: 8; z = z_hi * 8 + z_lo), core: 2. Of those that a mesh axis runs over, the one named last changes fastest.
Arguments:
- hidden: bfloat16 [8192, 5120], P('head', 'lat'), may hold values from -6 to 6
- w_down: bfloat16 [5120, 1536], P('lat', 'head'), may hold values from -0.078125 to 0.078125
- w_up: bfloat16 [1536, 24576], P('head', 'lat'), may hold values from -0.15625 to 0.15625
- norm_gain: float32 [1536], replicated, may hold values from 0.5 to 1.5
- cotangent: bfloat16 [8192, 24576], P('head', 'lat'), may hold values from -6 to 6
Outputs:
- queries: bfloat16 [8192, 24576], P('head', 'lat')
- dhidden: bfloat16 [8192, 5120], P('head', 'lat')
- dgain: float32 [1536], P('lat')
All inputs are finite; a program needn't handle non-finite values.
Results may differ from a plain program's by a relative error of at most 0.023.
Values may be sent and summed in bfloat16 or wider, within the bound.
A program may use at most 64 MiB of HBM per device.

v0:
```python
import jax
import jax.numpy as jnp
from jax import lax
from jax.sharding import PartitionSpec as P

R = 1536


def body(hidden, w_down, w_up, norm_gain, cotangent):
    lat_count = lax.axis_size("lat")
    lat_index = lax.axis_index("lat")
    share = R // lat_count
    down_full = lax.all_gather(w_down, "head", axis=1, tiled=True)
    partial_value = jnp.dot(hidden, down_full, preferred_element_type=jnp.float32).astype(
        jnp.bfloat16
    )
    latent = lax.psum_scatter(partial_value, "lat", scatter_dimension=1, tiled=True).astype(
        jnp.float32
    )
    squares = lax.psum(jnp.sum(latent * latent, axis=1), "lat")
    scales = lax.rsqrt(squares / R + 1e-06)
    gain_part = lax.dynamic_slice_in_dim(norm_gain, lat_index * share, share, 0)
    local_normed = (latent * scales[:, None] * gain_part).astype(jnp.bfloat16)
    normed = lax.all_gather(local_normed, "lat", axis=1, tiled=True)
    queries = jnp.dot(
        normed, lax.all_gather(w_up, "head", axis=0, tiled=True), preferred_element_type=jnp.float32
    )
    dpartial = lax.dot_general(
        cotangent,
        lax.all_gather(w_up, "head", axis=0, tiled=True),
        (((1,), (1,)), ((), ())),
        preferred_element_type=jnp.float32,
    )
    dpartial = dpartial.astype(jnp.bfloat16)
    dnormed = lax.psum_scatter(dpartial, "lat", scatter_dimension=1, tiled=True).astype(jnp.float32)
    weighted = gain_part * dnormed
    inner_sum = lax.psum(jnp.sum(weighted * latent, axis=1), "lat")
    dlocal = (scales[:, None] * weighted - latent * (scales**3 * inner_sum / R)[:, None]).astype(
        jnp.bfloat16
    )
    dlatent = lax.all_gather(dlocal, "lat", axis=1, tiled=True)
    gain_local = jnp.sum(dnormed * latent * scales[:, None], axis=0)
    dgain = lax.psum(gain_local, "head")
    dhidden = lax.dot_general(
        dlatent, down_full, (((1,), (1,)), ((), ())), preferred_element_type=jnp.float32
    )
    return (queries.astype(jnp.bfloat16), dhidden.astype(jnp.bfloat16), dgain)


def solution(mesh):
    placed = (P("head", "lat"), P("lat", "head"), P("head", "lat"), P(), P("head", "lat"))
    return jax.shard_map(
        body,
        mesh=mesh,
        in_specs=placed,
        out_specs=(P("head", "lat"), P("head", "lat"), P("lat")),
        check_vma=False,
    )
```

profile of v0, /device:TPU:1, one launch (start us, length us, event | category | flops | bytes accessed | tf_op | source)
XLA Modules:
  0.0 642.0 jit_solution(3078134584218905463)
XLA Ops:
  8.0 0.0 copy-start
  8.0 0.0 all-gather.2.cloned.1.call-start
  8.1 0.7 all-gather.2.cloned.1.call-update
  8.7 0.0 reduce-scatter.3.cloned.1.call-start
  8.8 123.6 %all_gather.13 = bf16[320,1536]{0,1:T(8,128)(2,1)S(1)} all-gather(bf16[320,48]{0,1:T(8,128)(2,1)} %param.6), channel_id=1, replica_groups=mesh['lat'=16,'head'=32] {'head'}, dimensions={1}, use_global_device_ids=true | all-gather | bytes 1013760 | tf_op jit(solution)/shard_map/all_gather | solution.py:13
  132.4 2.4 convolution_convert_fusion
  134.8 0.0 reduce-scatter.3.cloned.1.call-update
  134.8 0.0 reduce-scatter.5.cloned.1.call-start
  134.9 94.4 %all-gather.2.cloned.1.call-done = bf16[1536,1536]{1,0:T(8,128)(2,1)} async-done(((bf16[48,1536]{1,0:T(8,128)(2,1)}), bf16[1536,1536]{1,0:T(8,128)(2,1)}) %all-gather.2.cloned.1.call-update) | async-done | bytes 4718608 | tf_op jit(solution)/shard_map/all_gather | solution.py:26
  229.2 0.0 copy-done
  229.2 4.6 convolution_convert_fusion.1
  233.9 0.0 reduce-scatter.5.cloned.1.call-update
  233.9 0.8 dynamic_slice.3
  234.7 10.3 %reduce-scatter.3.cloned.1.call-done = bf16[256,96]{0,1:T(8,128)(2,1)} async-done(((bf16[256,1536]{0,1:T(8,128)(2,1)}), bf16[256,96]{0,1:T(8,128)(2,1)}) %reduce-scatter.3.cloned.1.call-update) | async-done | bytes 49168 | tf_op jit(solution)/shard_map/reduce_scatter | solution.py:17
  245.0 0.8 fusion.3
  245.8 75.6 %psum.21 = f32[256]{0:T(256)S(1)} all-reduce(f32[256]{0:T(256)S(1)} %fusion.3), channel_id=1, replica_groups=mesh['lat'=16,'head'=32] {'lat'}, use_global_device_ids=true, to_apply=%region_2.0 | all-reduce | flops 256 | bytes 2048 | tf_op jit(solution)/shard_map/psum | solution.py:20
  321.4 31.6 %reduce-scatter.5.cloned.1.call-done = bf16[256,96]{0,1:T(8,128)(2,1)} async-done(((bf16[256,1536]{0,1:T(8,128)(2,1)}), bf16[256,96]{0,1:T(8,128)(2,1)}) %reduce-scatter.5.cloned.1.call-update) | async-done | bytes 49168 | tf_op jit(solution)/shard_map/reduce_scatter | solution.py:35
  353.0 1.0 fusion.8
  354.1 101.7 %psum.23 = f32[96]{0:T(128)} all-reduce(f32[96]{0:T(128)S(1)} %get-tuple-element.3), channel_id=1, replica_groups=mesh['lat'=16,'head'=32] {'head'}, use_global_device_ids=true, to_apply=%region_7.0 | all-reduce | flops 96 | bytes 768 | tf_op jit(solution)/shard_map/psum | solution.py:43
  455.7 79.6 %psum.22 = f32[256]{0:T(256)S(1)} all-reduce(f32[256]{0:T(256)S(1)} %get-tuple-element.4), channel_id=1, replica_groups=mesh['lat'=16,'head'=32] {'lat'}, use_global_device_ids=true, to_apply=%region_5.0 | all-reduce | flops 256 | bytes 2048 | tf_op jit(solution)/shard_map/psum | solution.py:37
  535.4 0.9 fusion.2
  536.3 47.5 %all_gather.16 = bf16[256,1536]{0,1:T(8,128)(2,1)S(1)} all-gather(bf16[256,96]{0,1:T(8,128)(2,1)S(1)} %get-tuple-element.5), channel_id=1, replica_groups=mesh['lat'=16,'head'=32] {'lat'}, dimensions={1}, use_global_device_ids=true | all-gather | bytes 835584 | tf_op jit(solution)/shard_map/all_gather | solution.py:41
  583.7 1.2 convolution_convert_fusion.3
  585.0 45.0 %all_gather.14 = bf16[256,1536]{0,1:T(8,128)(2,1)S(1)} all-gather(bf16[256,96]{0,1:T(8,128)(2,1)S(1)} %get-tuple-element.6), channel_id=1, replica_groups=mesh['lat'=16,'head'=32] {'lat'}, dimensions={1}, use_global_device_ids=true | all-gather | bytes 835584 | tf_op jit(solution)/shard_map/all_gather | solution.py:24
  629.9 4.6 convolution_convert_fusion.2
  (2 shorter events, 0.0 us)
Async XLA Ops:
  8.0 221.2 %copy-start = (bf16[256,1536]{1,0:T(8,128)(2,1)S(1)}, bf16[256,1536]{1,0:T(8,128)(2,1)}, u32[]{:S(2)}) copy-start(bf16[256,1536]{1,0:T(8,128)(2,1)} %param.9) | copy-start | bytes 2359300
  8.0 221.2 %all-gather.2.cloned.1.call-start = ((), (), s32[]{:S(2)}) async-start(), calls=%async_computation.3 | async-start | bytes 4866048 | tf_op jit(solution)/shard_map/all_gather | solution.py:26
  8.7 236.2 %reduce-scatter.3.cloned.1.call-start = ((), (), s32[]{:S(2)}) async-start(), calls=%async_computation.2 | async-start | bytes 835584 | tf_op jit(solution)/shard_map/reduce_scatter | solution.py:17
  134.8 218.2 %reduce-scatter.5.cloned.1.call-start = ((), (), s32[]{:S(2)}) async-start(), calls=%async_computation.4 | async-start | bytes 835584 | tf_op jit(solution)/shard_map/reduce_scatter | solution.py:35
Sparse Core Ops, SparseCore 0:
  10.9 218.2 all-gather.1
Sparse Core Ops, SparseCore 1:
  134.9 110.0 reduce-scatter.2
  250.0 102.9 reduce-scatter.4
where the time goes:
time: 644 us; the launch traced here: 642 us
  blocking collectives  473 us (73%)
  waiting for transfers between devices  137 us (21%)
  between operations  15.5 us (2%)
  matrix products  12.8 us (2%)
    all_gather x1, blocking collectives, body(): down_full = lax.all_gather(w_down, 'head', axis=1, tiled=True)  124 us
    psum x1, blocking collectives, body(): dgain = lax.psum(gain_local, 'head')  102 us
    all_gather x1, waiting for transfers between devices, body(): lax.all_gather(w_up, 'head', axis=0, tiled=True)  94.4 us
    psum x1, blocking collectives, body(): inner_sum = lax.psum(jnp.sum(weighted * latent, axis=1), 'lat')  79.6 us
    psum x1, blocking collectives, body(): squares = lax.psum(jnp.sum(latent * latent, axis=1), 'lat')  75.6 us
    all_gather x1, blocking collectives, body(): dlatent = lax.all_gather(dlocal, 'lat', axis=1, tiled=True)  47.5 us
    all_gather x1, blocking collectives, body(): normed = lax.all_gather(local_normed, 'lat', axis=1, tiled=True)  45 us
    reduce_scatter x1, waiting for transfers between devices, body(): lax.psum_scatter(dpartial, 'lat', scatter_dimension=1, tiled=True)  31.6 us
  transfers between devices with their start and end apart: 3, of which 3 were waited for; matrix products, arithmetic and copies ran while one was open for 1% of the time, Pallas kernels for 0%

commit v1 on v0

v1 whole, which is shorter than its diff:
```python
import jax
import jax.numpy as jnp
from jax import lax
from jax.experimental import pallas as pl
from jax.experimental.pallas import tpu as pltpu
from jax.sharding import PartitionSpec as P

MESH = pl.DeviceIdType.MESH
R = 1536
ROWS = 48
TOK = 256
FEAT = 320
COLS = 1536
CH = 384
F32 = jnp.float32
BF16 = jnp.bfloat16


def kernel(
    hid, wd_in, wu_in, gain, cot,
    q_out, dh_out, dg_out,
    WU, WD, DP, RC, S1, RY, S2, RZ, RES, AG, SC, GS, GR,
    loc, zr, zsu, zsd, xr, xsp, xsm, rel,
    wzr, wzs, wxr, wxp, wxm, wrel,
    cs, cr, ys, yr, hs, hr,
    ahs, ahr, ays, ayr, acs, acr, gs, gr,
):
    lat = lax.axis_index("lat")
    head = lax.axis_index("head")
    x, z = head % 4, head // 4
    y, zh, c = lat // 4, (lat // 2) % 2, lat % 2

    def xdev(d):
        return (lat, z * 4 + (x + d) % 4)

    def zdev(zt):
        return (lat, zt * 4 + x)

    def ydev(d):
        return (((y + d) % 4) * 4 + zh * 2 + c, head)

    cdev = (y * 4 + zh * 2 + (1 - c), head)
    hdev = (y * 4 + (1 - zh) * 2 + c, head)

    def copy(src, dst, ss, rs, dev):
        return pltpu.make_async_remote_copy(
            src_ref=src, dst_ref=dst, send_sem=ss, recv_sem=rs, device_id=dev, device_id_type=MESH
        )

    def send(src, dst, ss, rs, dev):
        copy(src, dst, ss, rs, dev).start()

    def arrived(dst, rs):
        copy(dst, dst, rs, rs, cdev).wait_recv()

    def left(src, ss):
        copy(src, src, ss, ss, cdev).wait_send()

    bar = pltpu.get_barrier_semaphore()
    partners = [xdev(d) for d in (1, 2, 3)] + [ydev(d) for d in (1, 2, 3)] + [cdev, hdev]
    partners += [zdev((z + d) % 8) for d in range(1, 8)]
    for dev in partners:
        pl.semaphore_signal(bar, inc=1, device_id=dev, device_id_type=MESH)
    pl.semaphore_wait(bar, len(partners))

    me = head
    ZORDER = (1, 7, 2, 6, 3, 5, 4)
    for d in ZORDER:
        send(wd_in, WD.at[me], wzs.at[d - 1], wzr.at[z], zdev((z + d) % 8))
    send(wd_in, WD.at[me], wxp.at[z], wxr.at[me], xdev(1))
    send(wd_in, WD.at[me], wxm.at[z], wxr.at[me], xdev(3))
    for k in range(3):
        rows = pl.ds(16 * k, 16)

        @pl.when(z < 7)
        def _():
            send(wu_in.at[rows], WU.at[me, rows], zsu.at[z, k], zr.at[z, k], zdev(jnp.minimum(z + 1, 7)))

        @pl.when(z > 0)
        def _():
            send(wu_in.at[rows], WU.at[me, rows], zsd.at[z, k], zr.at[z, k], zdev(jnp.maximum(z - 1, 0)))

    send(wu_in, WU.at[me], xsp.at[z], xr.at[me], xdev(1))
    send(wu_in, WU.at[me], xsm.at[z], xr.at[me], xdev(3))
    own_u = pltpu.make_async_copy(wu_in, WU.at[me], loc.at[0])
    own_d = pltpu.make_async_copy(wd_in, WD.at[me], loc.at[1])
    own_u.start()
    own_d.start()
    own_u.wait()
    own_d.wait()

    for d in ZORDER:
        zs = (z + d) % 8
        b = zs * 4 + x
        arrived(WD.at[b], wzr.at[zs])
        send(WD.at[b], WD.at[b], wxp.at[zs], wxr.at[b], xdev(1))
        send(WD.at[b], WD.at[b], wxm.at[zs], wxr.at[b], xdev(3))

    def relay_of(zs):
        even = 1 - zs % 2
        from_left, from_right = (x + 3) % 4, (x + 1) % 4
        first = even * from_left + (1 - even) * from_right
        other = even * from_right + (1 - even) * from_left
        return zs * 4 + first, zs * 4 + other, (lat, z * 4 + other)

    def wd_relay(i, _):
        zs = (z + i) % 8
        first, _o, dev = relay_of(zs)
        arrived(WD.at[first], wxr.at[first])
        send(WD.at[first], WD.at[first], wrel.at[zs], wxr.at[first], dev)
        return 0

    def wd_rest(i, _):
        zs = (z + i) % 8
        _f, other, _d = relay_of(zs)
        far = zs * 4 + (x + 2) % 4
        arrived(WD.at[other], wxr.at[other])
        arrived(WD.at[far], wxr.at[far])
        return 0

    def take(zs, up):
        b = zs * 4 + x
        for k in range(3):
            rows = pl.ds(16 * k, 16)
            arrived(WU.at[b, rows], zr.at[zs, k])
            if up:
                @pl.when(z < 7)
                def _():
                    send(WU.at[b, rows], WU.at[b, rows], zsu.at[zs, k], zr.at[zs, k], zdev(jnp.minimum(z + 1, 7)))
            else:
                @pl.when(z > 0)
                def _():
                    send(WU.at[b, rows], WU.at[b, rows], zsd.at[zs, k], zr.at[zs, k], zdev(jnp.maximum(z - 1, 0)))
        send(WU.at[b], WU.at[b], xsp.at[zs], xr.at[b], xdev(1))
        send(WU.at[b], WU.at[b], xsm.at[zs], xr.at[b], xdev(3))

    def both(s, f):
        lo, hi = z - s, z + s

        @pl.when((s >= 0) & (lo >= 0))
        def _():
            f(jnp.maximum(lo, 0), True)

        @pl.when((s >= 1) & (hi <= 7))
        def _():
            f(jnp.minimum(hi, 7), False)

    def relay(zs, up):
        first, _o, dev = relay_of(zs)
        arrived(WU.at[first], xr.at[first])
        send(WU.at[first], WU.at[first], rel.at[zs], xr.at[first], dev)

    def rest(zs, up):
        _f, other, _d = relay_of(zs)
        far = zs * 4 + (x + 2) % 4
        arrived(WU.at[other], xr.at[other])
        arrived(WU.at[far], xr.at[far])

    c_own = pl.ds(pl.multiple_of(c * 128, 128), 128)
    c_other = pl.ds(pl.multiple_of((1 - c) * 128, 128), 128)

    def y_rows(yt):
        return pl.ds(pl.multiple_of(yt * 32, 32), 32)

    h_own = pl.ds(pl.multiple_of(zh * 16, 16), 16)
    h_other = pl.ds(pl.multiple_of((1 - zh) * 16, 16), 16)

    def sum0(j, value):
        DP[j] = value.astype(BF16)
        send(DP.at[j, c_other], RC.at[j], cs.at[j], cr.at[j], cdev)

    def sum1(j):
        arrived(RC.at[j], cr.at[j])
        S1[j] = (DP[j, c_own].astype(F32) + RC[j].astype(F32)).astype(BF16)
        for d in (2, 1, 3):
            send(S1.at[j, y_rows((y + d) % 4)], RY.at[j, d - 1], ys.at[j, d - 1], yr.at[j, d - 1], ydev(d))

    def sum2(j):
        total = S1[j, y_rows(y)].astype(F32)
        for d in (1, 3, 2):
            arrived(RY.at[j, d - 1], yr.at[j, d - 1])
            total = total + RY[j, d - 1].astype(F32)
        S2[j] = total.astype(BF16)
        send(S2.at[j, h_other], RZ.at[j], hs.at[j], hr.at[j], hdev)

    def sum3(j):
        arrived(RZ.at[j], hr.at[j])
        RES[j] = S2[j, h_own].astype(F32) + RZ[j].astype(F32)

    def each(f):
        lax.fori_loop(0, 4, lambda q, v: (f(q), v)[1], 0)

    nt = (((1,), (1,)), ((), ()))

    def down(q):
        w = WD[pl.ds(8 * q, 8)].reshape(CH, FEAT)
        sum0(q, lax.dot_general(hid[...], w, nt, preferred_element_type=F32))

    def up_back(q):
        w = WU[pl.ds(8 * q, 8)].reshape(CH, COLS)
        sum0(4 + q, lax.dot_general(cot[...], w, nt, preferred_element_type=F32))

    def tok(yt, ht):
        return pl.ds(pl.multiple_of(c * 128 + yt * 32 + ht * 16, 16), 16)

    def gather1(k):
        rows = tok(y, zh)
        send(AG.at[k, rows], AG.at[k, rows], ahs.at[k], ahr.at[k], hdev)
        for d in (2, 1, 3):
            send(AG.at[k, rows], AG.at[k, rows], ays.at[k, 0, d - 1], ayr.at[k, 0, d - 1], ydev(d))

    def gather2(k):
        rows = tok(y, 1 - zh)
        arrived(AG.at[k, rows], ahr.at[k])
        for d in (2, 1, 3):
            send(AG.at[k, rows], AG.at[k, rows], ays.at[k, 1, d - 1], ayr.at[k, 1, d - 1], ydev(d))

    def gather3(k):
        for d in (1, 3, 2):
            yt = (y + 4 - d) % 4
            arrived(AG.at[k, tok(yt, zh)], ayr.at[k, 0, d - 1])
            arrived(AG.at[k, tok(yt, 1 - zh)], ayr.at[k, 1, d - 1])
        send(AG.at[k, c_own], AG.at[k, c_own], acs.at[k], acr.at[k], cdev)

    def gather4(k):
        arrived(AG.at[k, c_other], acr.at[k])

    mine = tok(y, zh)

    def norm():
        squares = jnp.zeros((16, 1), F32)
        for q in range(4):
            v = RES[q]
            squares = squares + jnp.sum(v * v, axis=1, keepdims=True)
        scales = lax.rsqrt(squares / R + 1e-06)
        SC[...] = jnp.broadcast_to(scales, (16, 128))
        for q in range(4):
            cols = slice(q * CH, (q + 1) * CH)
            AG[0, mine, cols] = (RES[q] * scales * gain[:, cols]).astype(BF16)

    def back_norm():
        scales = SC[:, 0:1]
        inner = jnp.zeros((16, 1), F32)
        for q in range(4):
            cols = slice(q * CH, (q + 1) * CH)
            inner = inner + jnp.sum(gain[:, cols] * RES[4 + q] * RES[q], axis=1, keepdims=True)
        factor = scales * scales * scales * inner / R
        for q in range(4):
            cols = slice(q * CH, (q + 1) * CH)
            dn, latent = RES[4 + q], RES[q]
            AG[1, mine, cols] = (scales * (gain[:, cols] * dn) - latent * factor).astype(BF16)
            GS[0, :, cols] = jnp.sum(dn * latent * scales, axis=0, keepdims=True)

    def chunk_at(s):
        odd = (s + z) % 2
        q = odd * ((s + z - 1 + 8) // 2 - 4) + (1 - odd) * ((z - s + 16) // 2 - 8)
        ok = (s >= 1) & (q >= 0) & (q <= 3)
        return ok, jnp.clip(q, 0, 3)

    def step(i, carry):
        @pl.when(i <= 6)
        def _():
            s = i + 1
            lo, hi = z - s, z + s

            @pl.when(lo >= 0)
            def _():
                take(jnp.maximum(lo, 0), True)

            @pl.when(hi <= 7)
            def _():
                take(jnp.minimum(hi, 7), False)

        @pl.when(i == 0)
        def _():
            lax.fori_loop(0, 8, wd_relay, 0)

        @pl.when(i == 1)
        def _():
            lax.fori_loop(0, 8, wd_rest, 0)
            each(down)

        both(i - 2, relay)
        both(i - 3, rest)

        @pl.when(i == 2)
        def _():
            each(sum1)

        @pl.when(i == 4)
        def _():
            each(sum2)

        @pl.when(i == 5)
        def _():
            each(sum3)
            norm()
            gather1(0)

        @pl.when(i == 6)
        def _():
            gather2(0)

        @pl.when(i == 8)
        def _():
            gather3(0)

        for lag, f in ((3, sum3), (2, sum2), (1, sum1)):
            ok, q = chunk_at(i - 3 - lag)

            @pl.when(ok)
            def _():
                f(4 + q)

        ok, q = chunk_at(i - 3)

        @pl.when(ok)
        def _():
            up_back(q)

        return carry

    lax.fori_loop(0, 14, step, 0)

    back_norm()
    gather1(1)
    send(GS.at[0], GR.at[0], gs.at[0], gr.at[0], hdev)
    gather4(0)

    def queries(n):
        cols = slice(n * CH, (n + 1) * CH)
        w = WU[:, :, cols].reshape(R, CH)
        q_out[:, cols] = jnp.dot(AG[0], w, preferred_element_type=F32).astype(BF16)

    queries(0)
    queries(1)
    arrived(GR.at[0], gr.at[0])
    GS[1] = GS[0] + GR[0]
    gather2(1)
    for d in (1, 2, 3):
        send(GS.at[1], GR.at[d], gs.at[d], gr.at[d], ydev(d))
    queries(2)
    queries(3)
    total = GS[1]
    for d in (1, 2, 3):
        arrived(GR.at[d], gr.at[d])
        total = total + GR[d]
    GS[2] = total
    gather3(1)
    send(GS.at[2], GR.at[4], gs.at[4], gr.at[4], cdev)
    arrived(GR.at[4], gr.at[4])
    GS[3] = GS[2] + GR[4]
    for d in (1, 2, 3):
        send(GS.at[3], GR.at[4 + d], gs.at[4 + d], gr.at[4 + d], xdev(d))
    gather4(1)
    dh_out[...] = jnp.dot(AG[1], WD[...].reshape(R, FEAT), preferred_element_type=F32).astype(BF16)
    total = GS[3]
    for d in (1, 2, 3):
        arrived(GR.at[4 + d], gr.at[4 + d])
        total = total + GR[4 + d]
    GS[4] = total
    for d in range(1, 8):
        send(GS.at[4], GR.at[7 + d], gs.at[7 + d], gr.at[7 + d], zdev((z + d) % 8))
    for d in range(1, 8):
        arrived(GR.at[7 + d], gr.at[7 + d])
        total = total + GR[7 + d]
    dg_out[...] = total

    for d in range(1, 8):
        left(wd_in, wzs.at[d - 1])
    for zs in range(8):
        left(wd_in, wxp.at[zs])
        left(wd_in, wxm.at[zs])
        left(wd_in, wrel.at[zs])
        left(wu_in, xsp.at[zs])
        left(wu_in, xsm.at[zs])
        left(wu_in, rel.at[zs])
        for k in range(3):
            rows = pl.ds(16 * k, 16)

            @pl.when((zs <= z) & (z < 7))
            def _():
                left(wu_in.at[rows], zsu.at[zs, k])

            @pl.when((zs >= z) & (z > 0))
            def _():
                left(wu_in.at[rows], zsd.at[zs, k])

    def sums_left(j, v):
        left(RC.at[j], cs.at[j])
        for d in range(3):
            left(RY.at[j, d], ys.at[j, d])
        left(RZ.at[j], hs.at[j])
        return v

    lax.fori_loop(0, 8, sums_left, 0)
    for k in range(2):
        left(AG.at[k, mine], ahs.at[k])
        for d in range(3):
            left(AG.at[k, mine], ays.at[k, 0, d])
            left(AG.at[k, mine], ays.at[k, 1, d])
        left(AG.at[k, c_own], acs.at[k])
    for d in range(15):
        left(GS.at[0], gs.at[d])


def body(hidden, w_down, w_up, norm_gain, cotangent):
    vmem = pl.BlockSpec(memory_space=pltpu.VMEM)
    dma = pltpu.SemaphoreType.DMA
    queries, dhidden, dgain = pl.pallas_call(
        kernel,
        name="query_path",
        out_shape=(
            jax.ShapeDtypeStruct((TOK, COLS), BF16),
            jax.ShapeDtypeStruct((TOK, FEAT), BF16),
            jax.ShapeDtypeStruct((1, R), F32),
        ),
        in_specs=[vmem] * 5,
        out_specs=(vmem,) * 3,
        scratch_shapes=[
            pltpu.VMEM((32, ROWS, COLS), BF16),
            pltpu.VMEM((32, ROWS, FEAT), BF16),
            pltpu.VMEM((8, TOK, CH), BF16),
            pltpu.VMEM((8, 128, CH), BF16),
            pltpu.VMEM((8, 128, CH), BF16),
            pltpu.VMEM((8, 3, 32, CH), BF16),
            pltpu.VMEM((8, 32, CH), BF16),
            pltpu.VMEM((8, 16, CH), BF16),
            pltpu.VMEM((8, 16, CH), F32),
            pltpu.VMEM((2, TOK, R), BF16),
            pltpu.VMEM((16, 128), F32),
            pltpu.VMEM((5, 1, R), F32),
            pltpu.VMEM((15, 1, R), F32),
            dma((2,)), dma((8, 3)), dma((8, 3)), dma((8, 3)), dma((32,)), dma((8,)), dma((8,)), dma((8,)),
            dma((8,)), dma((7,)), dma((32,)), dma((8,)), dma((8,)), dma((8,)),
            dma((8,)), dma((8,)), dma((8, 3)), dma((8, 3)), dma((8,)), dma((8,)),
            dma((2,)), dma((2,)), dma((2, 2, 3)), dma((2, 2, 3)), dma((2,)), dma((2,)), dma((15,)), dma((15,)),
        ],
        compiler_params=pltpu.CompilerParams(
            collective_id=0, has_side_effects=True, vmem_limit_bytes=48 * 2**20
        ),
    )(hidden, w_down.T, w_up, norm_gain.reshape(1, R), cotangent)
    share = R // lax.axis_size("lat")
    dgain = lax.dynamic_slice_in_dim(dgain.reshape(R), lax.axis_index("lat") * share, share, 0)
    return queries, dhidden, dgain


def solution(mesh):
    placed = (P("head", "lat"), P("lat", "head"), P("head", "lat"), P(), P("head", "lat"))
    return jax.shard_map(
        body,
        mesh=mesh,
        in_specs=placed,
        out_specs=(P("head", "lat"), P("head", "lat"), P("lat")),
        check_vma=False,
    )
```

time: 644 us -> 148 us (0.23)
  blocking collectives: 473 us -> 0 us
  Pallas kernels: 0 us -> 141 us
  waiting for transfers between devices: 137 us -> 0 us
  between operations: 15.5 us -> 0.68 us
  matrix products: 12.8 us -> 0 us
    psum x3 -> x0, blocking collectives: 257 us -> none  [the longest x1 102 us: body(): dgain = lax.psum(gain_local, 'head')]
    all_gather x3 -> x0, blocking collectives: 216 us -> none  [the longest x1 124 us: body(): down_full = lax.all_gather(w_down, 'head', axis=1, tiled=True)]
    pallas_call x0 -> x1, Pallas kernels: none -> 141 us  [body(): pl.pallas_call(kernel, name='query_path', out_shape=(jax.ShapeDtypeStruct...]
    all_gather x1 -> x0, waiting for transfers between devices: 94.4 us -> none  [body(): lax.all_gather(w_up, 'head', axis=0, tiled=True)]
    reduce_scatter x2 -> x0, waiting for transfers between devices: 41.9 us -> none  [the longest x1 31.6 us: body(): lax.psum_scatter(dpartial, 'lat', scatter_dimension=1, tiled=True)]
    dot_general x4 -> x0, matrix products: 12.8 us -> none  [the longest x1 4.63 us: body(): lax.dot_general(cotangent, lax.all_gather(w_up, 'head', axis=0, tiled=Tru...]
  transfers between devices with their start and end apart: 3 -> 0, of which waited for: 3 -> 0; matrix products, arithmetic and copies ran while one was open for 1% -> 0% of each run, Pallas kernels for 0% -> 0%
where the time goes in v1:
time: 148 us; the launch traced here: 147 us
  Pallas kernels  141 us (95%)
  local copies, waits for them, and re-layouts  5.21 us (4%)
    pallas_call x1, Pallas kernels, body(): pl.pallas_call(kernel, name='query_path', out_shape=(jax.ShapeDtypeStruct...  141 us
    unnamed x11, local copies, waits for them, and re-layouts  4.62 us

profile of v1, /device:TPU:1, one launch (start us, length us, event | category | flops | bytes accessed | tf_op | source)
XLA Modules:
  0.0 147.3 jit_solution(8007689093035048937)
XLA Ops:
  0.6 0.0 copy-start.3
  0.6 0.7 copy-done.3
  1.3 0.0 copy-start.1
  1.3 0.0 copy-start.2
  1.3 1.1 copy.8.hid
  2.5 0.0 copy-done.1
  2.5 0.0 copy-done.2
  2.5 0.0 copy-start
  2.5 1.1 copy-done
  3.6 141.4 %query_path.1 = (bf16[256,1536]{1,0:T(8,128)(2,1)S(1)}, bf16[256,320]{1,0:T(8,128)(2,1)S(1)}, f32[1,1536]{1,0:T(1,128)S(1)}) custom-call(bf16[256,320]{1,0:T(8,128)(2,1)S(1)} %copy.8.hid, bf16[48,320]{1,0:T(8,128)(2,1)S(1)} %bitcast.3, bf16[48,1536]{1,0:T(8,128)(2,1)S(1)} %copy-done.1, f32[1,1536]{1,0:T(1,128)S(1)} %reshape.11.gain, ...), custom_call_target="tpu_custom_call" | custom-call | tf_op jit(solution)/shard_map/query_path/pallas_call | solution.py:410
  145.1 0.6 dynamic-slice_bitcast_fusion
  145.6 0.8 copy.9
  146.4 0.9 copy.11
  (1 shorter events, 0.0 us)
Async XLA Ops:
  0.6 0.7 copy-start.3
  1.3 1.1 copy-start.1
  1.3 1.1 copy-start.2
  2.5 1.1 copy-start

commit v2 on v0

v2 whole, which is shorter than its diff:
```python
import jax
import jax.numpy as jnp
from jax import lax
from jax.experimental import pallas as pl
from jax.experimental.pallas import tpu as pltpu
from jax.sharding import PartitionSpec as P

MESH = pl.DeviceIdType.MESH
R = 1536
ROWS = 48
TOK = 256
FEAT = 320
COLS = 1536
CH = 384
F32 = jnp.float32
BF16 = jnp.bfloat16
NT = (((1,), (1,)), ((), ()))


def unit(n):
    rows, cols = (lax.broadcasted_iota(jnp.int32, (n, n), d) for d in (0, 1))
    return (rows == cols).astype(BF16)


def kernel(
    hid_in, wd_in, wu_in, gain_in, cot_in,
    q_out, dh_out, dg_out,
    hid, hid_v, gain_v, gain, cot, qv,
    WU, WD, DP, RC, S1, RY, S2, RZ, RES, AGN, AGE, DL, SC, IG, INN, GS, GR,
    loc, zr, zsu, zsd, xr, xsp, xsm, rel,
    wzr, wzsu, wzsd, wxr, wxp, wxm, wrel,
    cs, cr, ys, yr, hs, hr,
    ays, ayr, acs, acr, gs, gr,
):
    lat = lax.axis_index("lat")
    head = lax.axis_index("head")
    x, z = head % 4, head // 4
    y, zh, c = lat // 4, (lat // 2) % 2, lat % 2

    def xdev(d):
        return (lat, z * 4 + (x + d) % 4)

    def zdev(zt):
        return (lat, zt * 4 + x)

    def ydev(d, core=c):
        return (((y + d) % 4) * 4 + zh * 2 + core, head)

    cdev = (y * 4 + zh * 2 + (1 - c), head)
    hdev = (y * 4 + (1 - zh) * 2 + c, head)
    group = [ydev(1), ydev(2), ydev(3), cdev, ydev(1, 1 - c), ydev(2, 1 - c), ydev(3, 1 - c)]

    def copy(src, dst, ss, rs, dev):
        return pltpu.make_async_remote_copy(
            src_ref=src, dst_ref=dst, send_sem=ss, recv_sem=rs, device_id=dev, device_id_type=MESH
        )

    def send(src, dst, ss, rs, dev):
        copy(src, dst, ss, rs, dev).start()

    def arrived(dst, rs):
        copy(dst, dst, rs, rs, cdev).wait_recv()

    def left(src, ss):
        copy(src, src, ss, ss, cdev).wait_send()

    bar = pltpu.get_barrier_semaphore()
    partners = [xdev(d) for d in (1, 2, 3)] + group + [hdev]
    partners += [zdev((z + d) % 8) for d in range(1, 8)]
    for dev in partners:
        pl.semaphore_signal(bar, inc=1, device_id=dev, device_id_type=MESH)
    me = head
    inputs = [
        pltpu.make_async_copy(src, dst, loc.at[n])
        for n, (src, dst) in enumerate(
            ((wd_in, WD.at[me]), (wu_in, WU.at[me]), (hid_in, hid_v), (gain_in, gain_v), (cot_in, cot))
        )
    ]
    for cp in inputs:
        cp.start()
    for cp in inputs:
        cp.wait()
    hid[...] = lax.dot_general(unit(TOK), hid_v[...], NT, preferred_element_type=F32).astype(BF16)
    gain[...] = gain_v[...].reshape(1, R)
    IG[...] = 1.0 / gain[...]
    INN[...] = jnp.zeros_like(INN)
    pl.semaphore_wait(bar, len(partners))

    def pass_up(zs, b, rows, k):
        @pl.when(z < 7)
        def _():
            send(WU.at[b, rows], WU.at[b, rows], zsu.at[zs, k], zr.at[zs, k], zdev(jnp.minimum(z + 1, 7)))

    def pass_down(zs, b, rows, k):
        @pl.when(z > 0)
        def _():
            send(WU.at[b, rows], WU.at[b, rows], zsd.at[zs, k], zr.at[zs, k], zdev(jnp.maximum(z - 1, 0)))

    def wd_up(zs, b):
        @pl.when(z < 7)
        def _():
            send(WD.at[b], WD.at[b], wzsu.at[zs], wzr.at[zs], zdev(jnp.minimum(z + 1, 7)))

    def wd_down(zs, b):
        @pl.when(z > 0)
        def _():
            send(WD.at[b], WD.at[b], wzsd.at[zs], wzr.at[zs], zdev(jnp.maximum(z - 1, 0)))

    wd_up(z, me)
    wd_down(z, me)
    for k in range(3):
        pass_up(z, me, pl.ds(16 * k, 16), k)
        pass_down(z, me, pl.ds(16 * k, 16), k)

    def spread(zs, b):
        send(WU.at[b], WU.at[b], xsp.at[zs], xr.at[b], xdev(1))
        send(WU.at[b], WU.at[b], xsm.at[zs], xr.at[b], xdev(3))

    def wd_spread(zs, b):
        send(WD.at[b], WD.at[b], wxp.at[zs], wxr.at[b], xdev(1))
        send(WD.at[b], WD.at[b], wxm.at[zs], wxr.at[b], xdev(3))

    wd_spread(z, me)
    spread(z, me)

    def both(s, f):
        lo, hi = z - s, z + s

        @pl.when((s >= 0) & (lo >= 0))
        def _():
            f(jnp.clip(lo, 0, 7), True)

        @pl.when((s >= 1) & (hi <= 7))
        def _():
            f(jnp.clip(hi, 0, 7), False)

    def relay_of(zs):
        even = 1 - zs % 2
        from_left, from_right = (x + 3) % 4, (x + 1) % 4
        first = even * from_left + (1 - even) * from_right
        other = even * from_right + (1 - even) * from_left
        return zs * 4 + first, zs * 4 + other, (lat, z * 4 + other)

    def wd_take(zs, up):
        b = zs * 4 + x
        arrived(WD.at[b], wzr.at[zs])
        (wd_up if up else wd_down)(zs, b)
        wd_spread(zs, b)

    def wd_relay(zs):
        first, _o, dev = relay_of(zs)
        arrived(WD.at[first], wxr.at[first])
        send(WD.at[first], WD.at[first], wrel.at[zs], wxr.at[first], dev)

    def wd_rest(zs):
        _f, other, _d = relay_of(zs)
        far = zs * 4 + (x + 2) % 4
        arrived(WD.at[other], wxr.at[other])
        arrived(WD.at[far], wxr.at[far])

    def take(zs, up):
        b = zs * 4 + x
        for k in range(3):
            rows = pl.ds(16 * k, 16)
            arrived(WU.at[b, rows], zr.at[zs, k])
            (pass_up if up else pass_down)(zs, b, rows, k)

    def relay(zs):
        first, _o, dev = relay_of(zs)
        arrived(WU.at[first], xr.at[first])
        send(WU.at[first], WU.at[first], rel.at[zs], xr.at[first], dev)

    def rest(zs):
        _f, other, _d = relay_of(zs)
        far = zs * 4 + (x + 2) % 4
        arrived(WU.at[other], xr.at[other])
        arrived(WU.at[far], xr.at[far])

    c_own = pl.ds(pl.multiple_of(c * 128, 128), 128)
    c_other = pl.ds(pl.multiple_of((1 - c) * 128, 128), 128)

    def y_rows(yt):
        return pl.ds(pl.multiple_of(yt * 32, 32), 32)

    def sum0(j, value):
        DP[j] = value.astype(BF16)
        send(DP.at[j, c_other], RC.at[j], cs.at[j], cr.at[j], cdev)

    def sum1(j):
        arrived(RC.at[j], cr.at[j])
        S1[j] = (DP[j, c_own].astype(F32) + RC[j].astype(F32)).astype(BF16)
        for d in (2, 1, 3):
            send(S1.at[j, y_rows((y + d) % 4)], RY.at[j, d - 1], ys.at[j, d - 1], yr.at[j, d - 1], ydev(d))

    def sum2(j):
        total = S1[j, y_rows(y)].astype(F32)
        for d in (1, 3, 2):
            arrived(RY.at[j, d - 1], yr.at[j, d - 1])
            total = total + RY[j, d - 1].astype(F32)
        S2[j] = total.astype(BF16)
        send(S2.at[j], RZ.at[j], hs.at[j], hr.at[j], hdev)

    def sum3(j):
        arrived(RZ.at[j], hr.at[j])
        RES[j] = S2[j].astype(F32) + RZ[j].astype(F32)

    def each(f):
        lax.fori_loop(0, 4, lambda q, v: (f(q), v)[1], 0)

    def down(q):
        w = WD[pl.ds(8 * q, 8)].reshape(CH, FEAT)
        sum0(q, lax.dot_general(hid[...], w, NT, preferred_element_type=F32))

    def up_back(q):
        w = WU[pl.ds(8 * q, 8)].reshape(CH, COLS)
        sum0(4 + q, lax.dot_general(cot[...], w, NT, preferred_element_type=F32))

    def tok(yt):
        return pl.ds(pl.multiple_of(c * 128 + yt * 32, 32), 32)

    mine = tok(y)

    def gather1(m, part):
        for d in (2, 1, 3):
            send(part(mine), part(mine), ays.at[m, d - 1], ayr.at[m, d - 1], ydev(d))

    def gather2(m, part):
        for d in (1, 3, 2):
            arrived(part(tok((y + 4 - d) % 4)), ayr.at[m, d - 1])
        send(part(c_own), part(c_own), acs.at[m], acr.at[m], cdev)

    def gather3(m, part):
        arrived(part(c_other), acr.at[m])

    def fwd(rows):
        return AGN.at[rows]

    def bwd(q):
        return lambda rows: AGE.at[q, rows]

    def norm():
        squares = jnp.zeros((32, 1), F32)
        for q in range(4):
            v = RES[q]
            squares = squares + jnp.sum(v * v, axis=1, keepdims=True)
        scales = lax.rsqrt(squares / R + 1e-06)
        SC[...] = jnp.broadcast_to(scales, (32, 128))
        for q in range(4):
            cols = slice(q * CH, (q + 1) * CH)
            AGN[mine, cols] = (RES[q] * scales * gain[:, cols]).astype(BF16)

    def q_cols(q):
        return pl.ds(pl.multiple_of(q * CH, CH), CH)

    def back3(q):
        sum3(4 + q)
        dn = RES[4 + q]
        scales = SC[:, 0:1]
        AGE[q, mine] = (scales * (gain[:, q_cols(q)] * dn)).astype(BF16)
        gather1(1 + q, bwd(q))
        GS[0, :, q_cols(q)] = jnp.sum(dn * RES[q] * scales, axis=0, keepdims=True)

    def back5(q):
        gather3(1 + q, bwd(q))
        n = AGN[:, q_cols(q)].astype(F32) * IG[:, q_cols(q)]
        part = jnp.sum(AGE[q].astype(F32) * n, axis=1, keepdims=True)
        INN[...] = INN[...] + jnp.broadcast_to(part, (TOK, 128))

    near_z = jnp.minimum(z, 7 - z)
    sign = jnp.where(z < 4, 1, -1)

    def in_turn(n, f):
        two = z + jnp.where(n % 2 == 1, -1, 1) * ((n + 1) // 2)
        one = z + sign * (n - near_z)

        @pl.when((n >= 0) & (n <= 7))
        def _():
            f(jnp.clip(jnp.where(n <= 2 * near_z, two, one), 0, 7))

    def turn(zs):
        d = jnp.abs(zs - z)
        return jnp.where(d > near_z, d + near_z, 2 * d - jnp.where(zs < z, 1, 0))

    def ready(q):
        return jnp.maximum(turn(2 * q), turn(2 * q + 1))

    def queries(n):
        cols = slice(n * CH, (n + 1) * CH)
        w = WU[:, :, cols].reshape(R, CH)
        qv[:, cols] = jnp.dot(AGN[...], w, preferred_element_type=F32).astype(BF16)

    def gain_send(value, slot, dev):
        send(GS.at[value], GR.at[slot], gs.at[slot], gr.at[slot], dev)

    def gain_sum(value, slots):
        total = GS[value]
        for n in slots:
            arrived(GR.at[n], gr.at[n])
            total = total + GR[n]
        return total

    q_copy = pltpu.make_async_copy(qv, q_out, loc.at[5])

    def weights_left():
        for zs in range(8):
            left(WD.at[0], wxp.at[zs])
            left(WD.at[0], wxm.at[zs])
            left(WD.at[0], wrel.at[zs])
            left(WU.at[0], xsp.at[zs])
            left(WU.at[0], xsm.at[zs])
            left(WU.at[0], rel.at[zs])

            @pl.when((zs <= z) & (z < 7))
            def _():
                left(WD.at[0], wzsu.at[zs])
                for k in range(3):
                    left(WU.at[0, pl.ds(16 * k, 16)], zsu.at[zs, k])

            @pl.when((zs >= z) & (z > 0))
            def _():
                left(WD.at[0], wzsd.at[zs])
                for k in range(3):
                    left(WU.at[0, pl.ds(16 * k, 16)], zsd.at[zs, k])

    def sums_left(j, v):
        left(RC.at[j], cs.at[j])
        for d in range(3):
            left(RY.at[j, d], ys.at[j, d])
        left(RZ.at[j], hs.at[j])
        return v

    def done_at(q):
        n = ready(q)
        return 4 + n - jnp.where(n >= 5, 1, 0) - jnp.where(n == 7, 1, 0)

    def step(i, carry):
        def at(when, f, *args):
            @pl.when(i == when)
            def _():
                f(*args)

        def turns(table, f):
            for when, n in table:
                at(when, in_turn, jnp.int32(n), f)

        at(12, weights_left)
        at(14, queries, 0)
        at(14, queries, 1)

        @pl.when(i >= 1)
        def _():
            in_turn(i, lambda zs: spread(zs, zs * 4 + x))

        for when, d in ((0, 2), (1, 3), (2, 4), (3, 5), (3, 6), (4, 7)):
            at(when, both, d, wd_take)
        both(i + 1, take)
        turns(((0, 1), (1, 2), (2, 3), (3, 4), (4, 5), (4, 6), (5, 7)), wd_relay)
        turns(((2, 0), (3, 1), (4, 2), (5, 3), (6, 4), (7, 5), (7, 6), (8, 7)), relay)
        turns(((1, 0), (2, 1), (3, 2), (4, 3), (5, 4)), wd_rest)
        turns(((4, 0), (5, 1), (6, 2), (7, 3), (8, 4), (8, 5), (9, 6), (9, 7)), rest)
        turns(((6, 5), (6, 6), (6, 7)), wd_rest)
        at(6, first)
        at(7, second)
        at(8, third)

        def chunks(stages):
            def chunk(q, v):
                done = done_at(q)
                back = jnp.maximum(done + 3, 11)
                for when, f in stages(done, back):
                    at(when, f, q)
                return v

            lax.fori_loop(0, 4, chunk, 0)

        chunks(lambda done, back: (
            (done + 2, lambda q: sum2(4 + q)),
            (done + 1, lambda q: sum1(4 + q)),
            (done, up_back),
        ))
        at(11, fourth)
        at(12, fifth)
        at(13, sixth)
        chunks(lambda done, back: (
            (back + 2, back5),
            (back + 1, lambda q: gather2(1 + q, bwd(q))),
            (back, back3),
        ))

        @pl.when(i == 12)
        def _():
            for n, dev in enumerate(group):
                gain_send(0, n, dev)

        @pl.when(i == 13)
        def _():
            GS[1] = gain_sum(0, range(7))
            for d in (1, 2, 3):
                gain_send(1, 6 + d, xdev(d))

        return carry

    def first():
        each(down)

    def second():
        each(sum1)

    def third():
        each(sum2)

    def fourth():
        each(sum3)
        norm()
        gather1(0, fwd)

    def fifth():
        gather2(0, fwd)

    def sixth():
        gather3(0, fwd)

    both(1, wd_take)
    in_turn(0, wd_relay)
    lax.fori_loop(0, 15, step, 0)

    inner = INN[:, 0:1] / R
    for q in range(4):
        cols = slice(q * CH, (q + 1) * CH)
        n = AGN[:, cols].astype(F32) * IG[:, cols]
        DL[:, cols] = (AGE[q].astype(F32) - n * inner).astype(BF16)
    dh = jnp.dot(DL[...], WD[...].reshape(R, FEAT), preferred_element_type=F32).astype(BF16)
    dh_out[...] = lax.dot_general(unit(FEAT), dh, NT, preferred_element_type=F32).astype(BF16)
    GS[2] = gain_sum(1, range(7, 10))
    for d in range(1, 8):
        gain_send(2, 9 + d, zdev((z + d) % 8))
    queries(2)
    queries(3)
    q_copy.start()
    lax.fori_loop(0, 8, sums_left, 0)
    dg_out[...] = gain_sum(2, range(10, 17))
    q_copy.wait()

    for m in range(5):
        part = fwd if m == 0 else bwd(m - 1)
        for d in range(3):
            left(part(mine), ays.at[m, d])
        left(part(c_own), acs.at[m])
    for n in range(17):
        left(GS.at[0], gs.at[n])


def body(hidden, w_down, w_up, norm_gain, cotangent):
    vmem = pl.BlockSpec(memory_space=pltpu.VMEM)
    hbm = pl.BlockSpec(memory_space=pltpu.HBM)
    dma = pltpu.SemaphoreType.DMA
    queries, dhidden, dgain = pl.pallas_call(
        kernel,
        name="query_path",
        out_shape=(
            jax.ShapeDtypeStruct((TOK, COLS), BF16),
            jax.ShapeDtypeStruct((FEAT, TOK), BF16),
            jax.ShapeDtypeStruct((1, R), F32),
        ),
        in_specs=[hbm] * 5,
        out_specs=(hbm, vmem, vmem),
        scratch_shapes=[
            pltpu.VMEM((TOK, FEAT), BF16),
            pltpu.VMEM((FEAT, TOK), BF16),
            pltpu.VMEM((R,), F32),
            pltpu.VMEM((1, R), F32),
            pltpu.VMEM((TOK, COLS), BF16),
            pltpu.VMEM((TOK, COLS), BF16),
            pltpu.VMEM((32, ROWS, COLS), BF16),
            pltpu.VMEM((32, ROWS, FEAT), BF16),
            pltpu.VMEM((8, TOK, CH), BF16),
            pltpu.VMEM((8, 128, CH), BF16),
            pltpu.VMEM((8, 128, CH), BF16),
            pltpu.VMEM((8, 3, 32, CH), BF16),
            pltpu.VMEM((8, 32, CH), BF16),
            pltpu.VMEM((8, 32, CH), BF16),
            pltpu.VMEM((8, 32, CH), F32),
            pltpu.VMEM((TOK, R), BF16),
            pltpu.VMEM((4, TOK, CH), BF16),
            pltpu.VMEM((TOK, R), BF16),
            pltpu.VMEM((32, 128), F32),
            pltpu.VMEM((1, R), F32),
            pltpu.VMEM((TOK, 128), F32),
            pltpu.VMEM((3, 1, R), F32),
            pltpu.VMEM((17, 1, R), F32),
            dma((6,)), dma((8, 3)), dma((8, 3)), dma((8, 3)), dma((32,)), dma((8,)), dma((8,)), dma((8,)),
            dma((8,)), dma((8,)), dma((8,)), dma((32,)), dma((8,)), dma((8,)), dma((8,)),
            dma((8,)), dma((8,)), dma((8, 3)), dma((8, 3)), dma((8,)), dma((8,)),
            dma((5, 3)), dma((5, 3)), dma((5,)), dma((5,)), dma((17,)), dma((17,)),
        ],
        compiler_params=pltpu.CompilerParams(
            collective_id=0, has_side_effects=True, vmem_limit_bytes=62 * 2**20
        ),
    )(hidden.T, w_down.T, w_up, norm_gain, cotangent)
    share = R // lax.axis_size("lat")
    dgain = lax.dynamic_slice_in_dim(dgain.reshape(R), lax.axis_index("lat") * share, share, 0)
    return queries, dhidden.T, dgain


def solution(mesh):
    placed = (P("head", "lat"), P("lat", "head"), P("head", "lat"), P(), P("head", "lat"))
    return jax.shard_map(
        body,
        mesh=mesh,
        in_specs=placed,
        out_specs=(P("head", "lat"), P("head", "lat"), P("lat")),
        check_vma=False,
    )
```

time: 644 us -> 108 us (0.17)
  blocking collectives: 473 us -> 0 us
  waiting for transfers between devices: 137 us -> 0 us
  Pallas kernels: 0 us -> 103 us
  between operations: 15.5 us -> 0.65 us
  matrix products: 12.8 us -> 0 us
    psum x3 -> x0, blocking collectives: 257 us -> none  [the longest x1 102 us: body(): dgain = lax.psum(gain_local, 'head')]
    all_gather x3 -> x0, blocking collectives: 216 us -> none  [the longest x1 124 us: body(): down_full = lax.all_gather(w_down, 'head', axis=1, tiled=True)]
    pallas_call x0 -> x1, Pallas kernels: none -> 103 us  [body(): pl.pallas_call(kernel, name='query_path', out_shape=(jax.ShapeDtypeStruct...]
    all_gather x1 -> x0, waiting for transfers between devices: 94.4 us -> none  [body(): lax.all_gather(w_up, 'head', axis=0, tiled=True)]
    reduce_scatter x2 -> x0, waiting for transfers between devices: 41.9 us -> none  [the longest x1 31.6 us: body(): lax.psum_scatter(dpartial, 'lat', scatter_dimension=1, tiled=True)]
    dot_general x4 -> x0, matrix products: 12.8 us -> none  [the longest x1 4.63 us: body(): lax.dot_general(cotangent, lax.all_gather(w_up, 'head', axis=0, tiled=Tru...]
  transfers between devices with their start and end apart: 3 -> 0, of which waited for: 3 -> 0; matrix products, arithmetic and copies ran while one was open for 1% -> 0% of each run, Pallas kernels for 0% -> 0%
where the time goes in v2:
time: 108 us
  Pallas kernels  103 us (95%)
  local copies, waits for them, and re-layouts  4.02 us (4%)
    pallas_call x1, Pallas kernels, body(): pl.pallas_call(kernel, name='query_path', out_shape=(jax.ShapeDtypeStruct...  103 us
    unnamed x4, local copies, waits for them, and re-layouts  2.77 us

profile of v2, /device:TPU:1, one launch (start us, length us, event | category | flops | bytes accessed | tf_op | source)
XLA Modules:
  0.0 107.6 jit_solution(12315602088029183066)
XLA Ops:
  0.6 102.9 %query_path.1 = (bf16[256,1536]{1,0:T(8,128)(2,1)}, bf16[320,256]{1,0:T(8,128)(2,1)}, f32[1,1536]{1,0:T(1,128)}) custom-call(bf16[320,256]{1,0:T(8,128)(2,1)} %bitcast.5, bf16[48,320]{1,0:T(8,128)(2,1)} %bitcast.7, bf16[48,1536]{1,0:T(8,128)(2,1)} %wu_in.1, f32[1536]{0:T(1024)} %gain_in.1, bf16[256,1536]{1,0:T(8,128)(2,1)} %cot_in.1), custom_call_target="tpu_custom_call" | custom-call | tf_op jit(solution)/shard_map/query_path/pallas_call | solution.py:457
  103.6 1.3 %dynamic-slice_bitcast_fusion = f32[96]{0:T(128)} fusion(f32[1,1536]{1,0:T(1,128)} %get-tuple-element.8, s32[]{:T(128)S(6)} %select_n.3), kind=kLoop, calls=%fused_computation | loop fusion | bytes 772 | tf_op jit(solution)/shard_map/dynamic_slice | solution.py:501
  104.8 0.0 copy-start
  104.9 2.1 %copy.10 = bf16[256,1536]{1,0:T(8,128)(2,1)} copy(bf16[256,1536]{1,0:T(8,128)(2,1)} %get-tuple-element.12) | data formatting | bytes 1572864
  107.0 0.0 copy-done
  107.0 0.7 copy.11
Async XLA Ops:
  104.8 2.1 %copy-start = (bf16[320,256]{1,0:T(8,128)(2,1)S(1)}, bf16[320,256]{1,0:T(8,128)(2,1)}, u32[]{:S(2)}) copy-start(bf16[320,256]{1,0:T(8,128)(2,1)} %get-tuple-element.7) | copy-start | bytes 491524

commit v3 on v2

--- a/solution.py
+++ b/solution.py
@@ -12,6 +12,7 @@
 FEAT = 320
 COLS = 1536
 CH = 384
+SHARE = 96
 F32 = jnp.float32
 BF16 = jnp.bfloat16
 NT = (((1,), (1,)), ((), ()))
@@ -25,12 +26,12 @@
 def kernel(
     hid_in, wd_in, wu_in, gain_in, cot_in,
     q_out, dh_out, dg_out,
-    hid, hid_v, gain_v, gain, cot, qv,
-    WU, WD, DP, RC, S1, RY, S2, RZ, RES, AGN, AGE, DL, SC, IG, INN, GS, GR,
+    hid, hid_v, gain_v, gain, cot, qv, dhv,
+    WU, WD, DP, RC, S1, RY, S2, RZ, RES, AGN, AGE, DL, SC, IG, INN, GS, GR, GZ,
     loc, zr, zsu, zsd, xr, xsp, xsm, rel,
     wzr, wzsu, wzsd, wxr, wxp, wxm, wrel,
     cs, cr, ys, yr, hs, hr,
-    ays, ayr, acs, acr, gs, gr,
+    ays, ayr, acs, acr, gs, gr, gzs, gzr,
 ):
     lat = lax.axis_index("lat")
     head = lax.axis_index("head")
@@ -43,12 +44,18 @@
     def zdev(zt):
         return (lat, zt * 4 + x)
 
-    def ydev(d, core=c):
-        return (((y + d) % 4) * 4 + zh * 2 + core, head)
+    def ydev(d):
+        return (((y + d) % 4) * 4 + zh * 2 + c, head)
 
     cdev = (y * 4 + zh * 2 + (1 - c), head)
     hdev = (y * 4 + (1 - zh) * 2 + c, head)
-    group = [ydev(1), ydev(2), ydev(3), cdev, ydev(1, 1 - c), ydev(2, 1 - c), ydev(3, 1 - c)]
+    group = []
+    for dx in range(4):
+        for dy in range(4):
+            for dc in range(2):
+                core = c + dc * (1 - 2 * c)
+                group.append((((y + dy) % 4) * 4 + zh * 2 + core, z * 4 + (x + dx) % 4))
+    group = group[1:]
 
     def copy(src, dst, ss, rs, dev):
         return pltpu.make_async_remote_copy(
@@ -65,7 +72,7 @@
         copy(src, src, ss, ss, cdev).wait_send()
 
     bar = pltpu.get_barrier_semaphore()
-    partners = [xdev(d) for d in (1, 2, 3)] + group + [hdev]
+    partners = group + [hdev]
     partners += [zdev((z + d) % 8) for d in range(1, 8)]
     for dev in partners:
         pl.semaphore_signal(bar, inc=1, device_id=dev, device_id_type=MESH)
@@ -116,6 +123,9 @@
         send(WU.at[b], WU.at[b], xsp.at[zs], xr.at[b], xdev(1))
         send(WU.at[b], WU.at[b], xsm.at[zs], xr.at[b], xdev(3))
 
+    def own_spread(zs):
+        spread(zs, zs * 4 + x)
+
     def wd_spread(zs, b):
         send(WD.at[b], WD.at[b], wxp.at[zs], wxr.at[b], xdev(1))
         send(WD.at[b], WD.at[b], wxm.at[zs], wxr.at[b], xdev(3))
@@ -289,16 +299,6 @@
         w = WU[:, :, cols].reshape(R, CH)
         qv[:, cols] = jnp.dot(AGN[...], w, preferred_element_type=F32).astype(BF16)
 
-    def gain_send(value, slot, dev):
-        send(GS.at[value], GR.at[slot], gs.at[slot], gr.at[slot], dev)
-
-    def gain_sum(value, slots):
-        total = GS[value]
-        for n in slots:
-            arrived(GR.at[n], gr.at[n])
-            total = total + GR[n]
-        return total
-
     q_copy = pltpu.make_async_copy(qv, q_out, loc.at[5])
 
     def weights_left():
@@ -333,71 +333,45 @@
         n = ready(q)
         return 4 + n - jnp.where(n >= 5, 1, 0) - jnp.where(n == 7, 1, 0)
 
+    def run_at(i, when, f, *args):
+        @pl.when(i == when)
+        def _():
+            f(*args)
+
+    def chunks(i, lag, earliest, f):
+        def chunk(q, v):
+            run_at(i, jnp.maximum(done_at(q) + lag, earliest), f, q)
+            return v
+
+        lax.fori_loop(0, 4, chunk, 0)
+
     def step(i, carry):
         def at(when, f, *args):
-            @pl.when(i == when)
-            def _():
-                f(*args)
+            run_at(i, when, f, *args)
 
         def turns(table, f):
             for when, n in table:
                 at(when, in_turn, jnp.int32(n), f)
 
-        at(12, weights_left)
-        at(14, queries, 0)
-        at(14, queries, 1)
-
-        @pl.when(i >= 1)
-        def _():
-            in_turn(i, lambda zs: spread(zs, zs * 4 + x))
-
+        turns(((1, 1), (2, 2), (3, 3), (4, 4)), own_spread)
         for when, d in ((0, 2), (1, 3), (2, 4), (3, 5), (3, 6), (4, 7)):
             at(when, both, d, wd_take)
         both(i + 1, take)
+        turns(((4, 5),), own_spread)
         turns(((0, 1), (1, 2), (2, 3), (3, 4), (4, 5), (4, 6), (5, 7)), wd_relay)
-        turns(((2, 0), (3, 1), (4, 2), (5, 3), (6, 4), (7, 5), (7, 6), (8, 7)), relay)
+        turns(((5, 6), (6, 7)), own_spread)
+        turns(((2, 0), (3, 1), (4, 2), (5, 3), (6, 4), (6, 5)), relay)
+        at(7, second)
+        turns(((7, 6), (7, 7)), relay)
         turns(((1, 0), (2, 1), (3, 2), (4, 3), (5, 4)), wd_rest)
-        turns(((4, 0), (5, 1), (6, 2), (7, 3), (8, 4), (8, 5), (9, 6), (9, 7)), rest)
+        turns(((4, 0), (5, 1), (6, 2), (7, 3), (8, 4), (8, 5)), rest)
+        at(8, third)
+        turns(((9, 6), (9, 7)), rest)
         turns(((6, 5), (6, 6), (6, 7)), wd_rest)
         at(6, first)
-        at(7, second)
-        at(8, third)
-
-        def chunks(stages):
-            def chunk(q, v):
-                done = done_at(q)
-                back = jnp.maximum(done + 3, 11)
-                for when, f in stages(done, back):
-                    at(when, f, q)
-                return v
-
-            lax.fori_loop(0, 4, chunk, 0)
-
-        chunks(lambda done, back: (
-            (done + 2, lambda q: sum2(4 + q)),
-            (done + 1, lambda q: sum1(4 + q)),
-            (done, up_back),
-        ))
-        at(11, fourth)
-        at(12, fifth)
-        at(13, sixth)
-        chunks(lambda done, back: (
-            (back + 2, back5),
-            (back + 1, lambda q: gather2(1 + q, bwd(q))),
-            (back, back3),
-        ))
-
-        @pl.when(i == 12)
-        def _():
-            for n, dev in enumerate(group):
-                gain_send(0, n, dev)
-
-        @pl.when(i == 13)
-        def _():
-            GS[1] = gain_sum(0, range(7))
-            for d in (1, 2, 3):
-                gain_send(1, 6 + d, xdev(d))
-
+        chunks(i, 0, 0, up_back)
+        chunks(i, 1, 0, lambda q: sum1(4 + q))
+        chunks(i, 2, 0, lambda q: sum2(4 + q))
         return carry
 
     def first():
@@ -422,32 +396,66 @@
 
     both(1, wd_take)
     in_turn(0, wd_relay)
-    lax.fori_loop(0, 15, step, 0)
-
+    lax.fori_loop(0, 10, step, 0)
+
+    chunks(10, 1, 0, lambda q: sum1(4 + q))
+    chunks(10, 2, 0, lambda q: sum2(4 + q))
+    weights_left()
+    chunks(11, 2, 0, lambda q: sum2(4 + q))
+    fourth()
+    chunks(11, 3, 11, back3)
+    chunks(12, 3, 11, back3)
+    for n, dev in enumerate(group):
+        send(GS.at[0], GR.at[n], gs.at[n], gr.at[n], dev)
+    fifth()
+    chunks(12, 4, 12, lambda q: gather2(1 + q, bwd(q)))
+    sixth()
+    queries(0)
+    queries(1)
+    chunks(13, 4, 12, lambda q: gather2(1 + q, bwd(q)))
+    total = GS[0]
+    for n in range(31):
+        arrived(GR.at[n], gr.at[n])
+        total = total + GR[n]
+    GS[1] = total
+    for k in range(16):
+        @pl.when(lat == k)
+        def _():
+            GZ[0] = GS[1, :, k * SHARE:(k + 1) * SHARE]
+
+    for d in range(1, 8):
+        send(GZ.at[0], GZ.at[d], gzs.at[d - 1], gzr.at[d - 1], zdev((z + d) % 8))
+    chunks(13, 5, 13, back5)
+    chunks(14, 5, 13, back5)
     inner = INN[:, 0:1] / R
     for q in range(4):
         cols = slice(q * CH, (q + 1) * CH)
         n = AGN[:, cols].astype(F32) * IG[:, cols]
         DL[:, cols] = (AGE[q].astype(F32) - n * inner).astype(BF16)
     dh = jnp.dot(DL[...], WD[...].reshape(R, FEAT), preferred_element_type=F32).astype(BF16)
-    dh_out[...] = lax.dot_general(unit(FEAT), dh, NT, preferred_element_type=F32).astype(BF16)
-    GS[2] = gain_sum(1, range(7, 10))
-    for d in range(1, 8):
-        gain_send(2, 9 + d, zdev((z + d) % 8))
+    dhv[...] = lax.dot_general(unit(FEAT), dh, NT, preferred_element_type=F32).astype(BF16)
+    dh_copy = pltpu.make_async_copy(dhv, dh_out, loc.at[0])
+    dh_copy.start()
     queries(2)
     queries(3)
     q_copy.start()
     lax.fori_loop(0, 8, sums_left, 0)
-    dg_out[...] = gain_sum(2, range(10, 17))
-    q_copy.wait()
-
     for m in range(5):
         part = fwd if m == 0 else bwd(m - 1)
         for d in range(3):
             left(part(mine), ays.at[m, d])
         left(part(c_own), acs.at[m])
-    for n in range(17):
+    for n in range(31):
         left(GS.at[0], gs.at[n])
+    share = GZ[0]
+    for d in range(1, 8):
+        arrived(GZ.at[d], gzr.at[d - 1])
+        share = share + GZ[d]
+    dg_out[...] = share
+    for d in range(7):
+        left(GZ.at[0], gzs.at[d])
+    q_copy.wait()
+    dh_copy.wait()
 
 
 def body(hidden, w_down, w_up, norm_gain, cotangent):
@@ -460,10 +468,10 @@
         out_shape=(
             jax.ShapeDtypeStruct((TOK, COLS), BF16),
             jax.ShapeDtypeStruct((FEAT, TOK), BF16),
-            jax.ShapeDtypeStruct((1, R), F32),
+            jax.ShapeDtypeStruct((1, SHARE), F32),
         ),
         in_specs=[hbm] * 5,
-        out_specs=(hbm, vmem, vmem),
+        out_specs=(hbm, hbm, vmem),
         scratch_shapes=[
             pltpu.VMEM((TOK, FEAT), BF16),
             pltpu.VMEM((FEAT, TOK), BF16),
@@ -471,6 +479,7 @@
             pltpu.VMEM((1, R), F32),
             pltpu.VMEM((TOK, COLS), BF16),
             pltpu.VMEM((TOK, COLS), BF16),
+            pltpu.VMEM((FEAT, TOK), BF16),
             pltpu.VMEM((32, ROWS, COLS), BF16),
             pltpu.VMEM((32, ROWS, FEAT), BF16),
             pltpu.VMEM((8, TOK, CH), BF16),
@@ -486,20 +495,19 @@
             pltpu.VMEM((32, 128), F32),
             pltpu.VMEM((1, R), F32),
             pltpu.VMEM((TOK, 128), F32),
-            pltpu.VMEM((3, 1, R), F32),
-            pltpu.VMEM((17, 1, R), F32),
+            pltpu.VMEM((2, 1, R), F32),
+            pltpu.VMEM((31, 1, R), F32),
+            pltpu.VMEM((8, 1, SHARE), F32),
             dma((6,)), dma((8, 3)), dma((8, 3)), dma((8, 3)), dma((32,)), dma((8,)), dma((8,)), dma((8,)),
             dma((8,)), dma((8,)), dma((8,)), dma((32,)), dma((8,)), dma((8,)), dma((8,)),
             dma((8,)), dma((8,)), dma((8, 3)), dma((8, 3)), dma((8,)), dma((8,)),
-            dma((5, 3)), dma((5, 3)), dma((5,)), dma((5,)), dma((17,)), dma((17,)),
+            dma((5, 3)), dma((5, 3)), dma((5,)), dma((5,)), dma((31,)), dma((31,)), dma((7,)), dma((7,)),
         ],
         compiler_params=pltpu.CompilerParams(
             collective_id=0, has_side_effects=True, vmem_limit_bytes=62 * 2**20
         ),
     )(hidden.T, w_down.T, w_up, norm_gain, cotangent)
-    share = R // lax.axis_size("lat")
-    dgain = lax.dynamic_slice_in_dim(dgain.reshape(R), lax.axis_index("lat") * share, share, 0)
-    return queries, dhidden.T, dgain
+    return queries, dhidden.T, dgain.reshape(SHARE)
 
 
 def solution(mesh):

time: 108 us -> 105 us (0.972)
  Pallas kernels: 103 us -> 101 us
    pallas_call x1, Pallas kernels: 103 us -> 101 us  [body(): pl.pallas_call(kernel, name='query_path', out_shape=(jax.ShapeDtypeStruct...]
    dynamic_slice x1 -> x0, local copies, waits for them, and re-layouts: 1.25 us -> none  [body(): lax.dynamic_slice_in_dim(dgain.reshape(R), lax.axis_index('lat') * share,...]
    unnamed x4 -> x7, local copies, waits for them, and re-layouts: 2.77 us -> 3.29 us
where the time goes in v3:
time: 105 us
  Pallas kernels  101 us (96%)
  local copies, waits for them, and re-layouts  3.29 us (3%)
    pallas_call x1, Pallas kernels, body(): pl.pallas_call(kernel, name='query_path', out_shape=(jax.ShapeDtypeStruct...  101 us
    unnamed x7, local copies, waits for them, and re-layouts  3.29 us

profile of v3, /device:TPU:1, one launch (start us, length us, event | category | flops | bytes accessed | tf_op | source)
XLA Modules:
  0.0 105.2 jit_solution(12916124023312760425)
XLA Ops:
  0.6 101.3 %query_path.1 = (bf16[256,1536]{1,0:T(8,128)(2,1)}, bf16[320,256]{1,0:T(8,128)(2,1)}, f32[1,96]{1,0:T(1,128)}) custom-call(bf16[320,256]{1,0:T(8,128)(2,1)} %bitcast.4, bf16[48,320]{1,0:T(8,128)(2,1)} %bitcast.6, bf16[48,1536]{1,0:T(8,128)(2,1)} %wu_in.1, f32[1536]{0:T(1024)} %gain_in.1, bf16[256,1536]{1,0:T(8,128)(2,1)} %cot_in.1), custom_call_target="tpu_custom_call" | custom-call | tf_op jit(solution)/shard_map/query_path/pallas_call | solution.py:465
  101.9 0.0 copy-start
  101.9 2.1 %copy.11 = bf16[256,1536]{1,0:T(8,128)(2,1)} copy(bf16[256,1536]{1,0:T(8,128)(2,1)} %get-tuple-element.12) | data formatting | bytes 1572864
  104.0 0.0 copy-done
  104.0 0.0 copy-start.1
  104.0 0.7 copy.12
  104.7 0.0 copy-done.1
  104.7 0.5 copy.13
Async XLA Ops:
  101.9 2.1 %copy-start = (bf16[320,256]{1,0:T(8,128)(2,1)S(1)}, bf16[320,256]{1,0:T(8,128)(2,1)}, u32[]{:S(2)}) copy-start(bf16[320,256]{1,0:T(8,128)(2,1)} %get-tuple-element.7) | copy-start | bytes 491524
  104.0 0.7 copy-start.1

commit v4 on v3

--- a/solution.py
+++ b/solution.py
@@ -28,8 +28,7 @@
     q_out, dh_out, dg_out,
     hid, hid_v, gain_v, gain, cot, qv, dhv,
     WU, WD, DP, RC, S1, RY, S2, RZ, RES, AGN, AGE, DL, SC, IG, INN, GS, GR, GZ,
-    loc, zr, zsu, zsd, xr, xsp, xsm, rel,
-    wzr, wzsu, wzsd, wxr, wxp, wxm, wrel,
+    loc, zr, zs_sem, xr, xs, wzr, wzs, wxr, wxs,
     cs, cr, ys, yr, hs, hr,
     ays, ayr, acs, acr, gs, gr, gzs, gzr,
 ):
@@ -96,22 +95,22 @@
     def pass_up(zs, b, rows, k):
         @pl.when(z < 7)
         def _():
-            send(WU.at[b, rows], WU.at[b, rows], zsu.at[zs, k], zr.at[zs, k], zdev(jnp.minimum(z + 1, 7)))
+            send(WU.at[b, rows], WU.at[b, rows], zs_sem, zr.at[zs, k], zdev(jnp.minimum(z + 1, 7)))
 
     def pass_down(zs, b, rows, k):
         @pl.when(z > 0)
         def _():
-            send(WU.at[b, rows], WU.at[b, rows], zsd.at[zs, k], zr.at[zs, k], zdev(jnp.maximum(z - 1, 0)))
+            send(WU.at[b, rows], WU.at[b, rows], zs_sem, zr.at[zs, k], zdev(jnp.maximum(z - 1, 0)))
 
     def wd_up(zs, b):
         @pl.when(z < 7)
         def _():
-            send(WD.at[b], WD.at[b], wzsu.at[zs], wzr.at[zs], zdev(jnp.minimum(z + 1, 7)))
+            send(WD.at[b], WD.at[b], wzs, wzr.at[zs], zdev(jnp.minimum(z + 1, 7)))
 
     def wd_down(zs, b):
         @pl.when(z > 0)
         def _():
-            send(WD.at[b], WD.at[b], wzsd.at[zs], wzr.at[zs], zdev(jnp.maximum(z - 1, 0)))
+            send(WD.at[b], WD.at[b], wzs, wzr.at[zs], zdev(jnp.maximum(z - 1, 0)))
 
     wd_up(z, me)
     wd_down(z, me)
@@ -120,15 +119,17 @@
         pass_down(z, me, pl.ds(16 * k, 16), k)
 
     def spread(zs, b):
-        send(WU.at[b], WU.at[b], xsp.at[zs], xr.at[b], xdev(1))
-        send(WU.at[b], WU.at[b], xsm.at[zs], xr.at[b], xdev(3))
+        even = 1 - zs % 2
+        send(WU.at[b], WU.at[b], xs, xr.at[zs + 8 * (1 - even)], xdev(1))
+        send(WU.at[b], WU.at[b], xs, xr.at[zs + 8 * even], xdev(3))
 
     def own_spread(zs):
         spread(zs, zs * 4 + x)
 
     def wd_spread(zs, b):
-        send(WD.at[b], WD.at[b], wxp.at[zs], wxr.at[b], xdev(1))
-        send(WD.at[b], WD.at[b], wxm.at[zs], wxr.at[b], xdev(3))
+        even = 1 - zs % 2
+        send(WD.at[b], WD.at[b], wxs, wxr.at[even * zs + 8 * (1 - even)], xdev(1))
+        send(WD.at[b], WD.at[b], wxs, wxr.at[(1 - even) * zs + 8 * even], xdev(3))
 
     wd_spread(z, me)
     spread(z, me)
@@ -149,7 +150,7 @@
         from_left, from_right = (x + 3) % 4, (x + 1) % 4
         first = even * from_left + (1 - even) * from_right
         other = even * from_right + (1 - even) * from_left
-        return zs * 4 + first, zs * 4 + other, (lat, z * 4 + other)
+        return zs * 4 + first, (lat, z * 4 + other)
 
     def wd_take(zs, up):
         b = zs * 4 + x
@@ -158,15 +159,9 @@
         wd_spread(zs, b)
 
     def wd_relay(zs):
-        first, _o, dev = relay_of(zs)
-        arrived(WD.at[first], wxr.at[first])
-        send(WD.at[first], WD.at[first], wrel.at[zs], wxr.at[first], dev)
-
-    def wd_rest(zs):
-        _f, other, _d = relay_of(zs)
-        far = zs * 4 + (x + 2) % 4
-        arrived(WD.at[other], wxr.at[other])
-        arrived(WD.at[far], wxr.at[far])
+        first, dev = relay_of(zs)
+        arrived(WD.at[first], wxr.at[zs])
+        send(WD.at[first], WD.at[first], wxs, wxr.at[8], dev)
 
     def take(zs, up):
         b = zs * 4 + x
@@ -176,15 +171,12 @@
             (pass_up if up else pass_down)(zs, b, rows, k)
 
     def relay(zs):
-        first, _o, dev = relay_of(zs)
-        arrived(WU.at[first], xr.at[first])
-        send(WU.at[first], WU.at[first], rel.at[zs], xr.at[first], dev)
+        first, dev = relay_of(zs)
+        arrived(WU.at[first], xr.at[zs])
+        send(WU.at[first], WU.at[first], xs, xr.at[8 + zs], dev)
 
     def rest(zs):
-        _f, other, _d = relay_of(zs)
-        far = zs * 4 + (x + 2) % 4
-        arrived(WU.at[other], xr.at[other])
-        arrived(WU.at[far], xr.at[far])
+        arrived(WU.at[pl.ds(0, 2)], xr.at[8 + zs])
 
     c_own = pl.ds(pl.multiple_of(c * 128, 128), 128)
     c_other = pl.ds(pl.multiple_of((1 - c) * 128, 128), 128)
@@ -194,21 +186,21 @@
 
     def sum0(j, value):
         DP[j] = value.astype(BF16)
-        send(DP.at[j, c_other], RC.at[j], cs.at[j], cr.at[j], cdev)
+        send(DP.at[j, c_other], RC.at[j], cs, cr.at[j], cdev)
 
     def sum1(j):
         arrived(RC.at[j], cr.at[j])
         S1[j] = (DP[j, c_own].astype(F32) + RC[j].astype(F32)).astype(BF16)
         for d in (2, 1, 3):
-            send(S1.at[j, y_rows((y + d) % 4)], RY.at[j, d - 1], ys.at[j, d - 1], yr.at[j, d - 1], ydev(d))
+            send(S1.at[j, y_rows((y + d) % 4)], RY.at[j, d - 1], ys, yr.at[j], ydev(d))
 
     def sum2(j):
         total = S1[j, y_rows(y)].astype(F32)
-        for d in (1, 3, 2):
-            arrived(RY.at[j, d - 1], yr.at[j, d - 1])
-            total = total + RY[j, d - 1].astype(F32)
+        arrived(RY.at[j], yr.at[j])
+        for d in range(3):
+            total = total + RY[j, d].astype(F32)
         S2[j] = total.astype(BF16)
-        send(S2.at[j], RZ.at[j], hs.at[j], hr.at[j], hdev)
+        send(S2.at[j], RZ.at[j], hs, hr.at[j], hdev)
 
     def sum3(j):
         arrived(RZ.at[j], hr.at[j])
@@ -232,12 +224,11 @@
 
     def gather1(m, part):
         for d in (2, 1, 3):
-            send(part(mine), part(mine), ays.at[m, d - 1], ayr.at[m, d - 1], ydev(d))
+            send(part(mine), part(mine), ays, ayr.at[m], ydev(d))
 
     def gather2(m, part):
-        for d in (1, 3, 2):
-            arrived(part(tok((y + 4 - d) % 4)), ayr.at[m, d - 1])
-        send(part(c_own), part(c_own), acs.at[m], acr.at[m], cdev)
+        arrived(part(pl.ds(0, 96)), ayr.at[m])
+        send(part(c_own), part(c_own), acs, acr.at[m], cdev)
 
     def gather3(m, part):
         arrived(part(c_other), acr.at[m])
@@ -302,32 +293,18 @@
     q_copy = pltpu.make_async_copy(qv, q_out, loc.at[5])
 
     def weights_left():
-        for zs in range(8):
-            left(WD.at[0], wxp.at[zs])
-            left(WD.at[0], wxm.at[zs])
-            left(WD.at[0], wrel.at[zs])
-            left(WU.at[0], xsp.at[zs])
-            left(WU.at[0], xsm.at[zs])
-            left(WU.at[0], rel.at[zs])
-
-            @pl.when((zs <= z) & (z < 7))
-            def _():
-                left(WD.at[0], wzsu.at[zs])
-                for k in range(3):
-                    left(WU.at[0, pl.ds(16 * k, 16)], zsu.at[zs, k])
-
-            @pl.when((zs >= z) & (z > 0))
-            def _():
-                left(WD.at[0], wzsd.at[zs])
-                for k in range(3):
-                    left(WU.at[0, pl.ds(16 * k, 16)], zsd.at[zs, k])
-
-    def sums_left(j, v):
-        left(RC.at[j], cs.at[j])
-        for d in range(3):
-            left(RY.at[j, d], ys.at[j, d])
-        left(RZ.at[j], hs.at[j])
-        return v
+        left(WU.at[pl.ds(0, 24)], xs)
+        left(WD.at[pl.ds(0, 24)], wxs)
+
+        @pl.when(near_z > 0)
+        def _():
+            left(WU.at[pl.ds(0, 9)], zs_sem)
+            left(WD.at[pl.ds(0, 9)], wzs)
+
+        @pl.when(near_z == 0)
+        def _():
+            left(WU.at[0], zs_sem)
+            left(WD.at[0], wzs)
 
     def done_at(q):
         n = ready(q)
@@ -363,11 +340,9 @@
         turns(((2, 0), (3, 1), (4, 2), (5, 3), (6, 4), (6, 5)), relay)
         at(7, second)
         turns(((7, 6), (7, 7)), relay)
-        turns(((1, 0), (2, 1), (3, 2), (4, 3), (5, 4)), wd_rest)
         turns(((4, 0), (5, 1), (6, 2), (7, 3), (8, 4), (8, 5)), rest)
         at(8, third)
         turns(((9, 6), (9, 7)), rest)
-        turns(((6, 5), (6, 6), (6, 7)), wd_rest)
         at(6, first)
         chunks(i, 0, 0, up_back)
         chunks(i, 1, 0, lambda q: sum1(4 + q))
@@ -375,6 +350,7 @@
         return carry
 
     def first():
+        arrived(WD.at[pl.ds(0, 16)], wxr.at[8])
         each(down)
 
     def second():
@@ -406,7 +382,7 @@
     chunks(11, 3, 11, back3)
     chunks(12, 3, 11, back3)
     for n, dev in enumerate(group):
-        send(GS.at[0], GR.at[n], gs.at[n], gr.at[n], dev)
+        send(GS.at[0], GR.at[n], gs, gr, dev)
     fifth()
     chunks(12, 4, 12, lambda q: gather2(1 + q, bwd(q)))
     sixth()
@@ -414,8 +390,8 @@
     queries(1)
     chunks(13, 4, 12, lambda q: gather2(1 + q, bwd(q)))
     total = GS[0]
+    arrived(GR, gr)
     for n in range(31):
-        arrived(GR.at[n], gr.at[n])
         total = total + GR[n]
     GS[1] = total
     for k in range(16):
@@ -424,7 +400,7 @@
             GZ[0] = GS[1, :, k * SHARE:(k + 1) * SHARE]
 
     for d in range(1, 8):
-        send(GZ.at[0], GZ.at[d], gzs.at[d - 1], gzr.at[d - 1], zdev((z + d) % 8))
+        send(GZ.at[0], GZ.at[d], gzs, gzr, zdev((z + d) % 8))
     chunks(13, 5, 13, back5)
     chunks(14, 5, 13, back5)
     inner = INN[:, 0:1] / R
@@ -439,21 +415,18 @@
     queries(2)
     queries(3)
     q_copy.start()
-    lax.fori_loop(0, 8, sums_left, 0)
-    for m in range(5):
-        part = fwd if m == 0 else bwd(m - 1)
-        for d in range(3):
-            left(part(mine), ays.at[m, d])
-        left(part(c_own), acs.at[m])
-    for n in range(31):
-        left(GS.at[0], gs.at[n])
+    left(RC, cs)
+    left(RY, ys)
+    left(RZ, hs)
+    left(AGN.at[pl.ds(0, 192)], ays)
+    left(AGN, acs)
+    left(GR, gs)
+    left(GZ.at[pl.ds(0, 7)], gzs)
+    arrived(GZ.at[pl.ds(1, 7)], gzr)
     share = GZ[0]
     for d in range(1, 8):
-        arrived(GZ.at[d], gzr.at[d - 1])
         share = share + GZ[d]
     dg_out[...] = share
-    for d in range(7):
-        left(GZ.at[0], gzs.at[d])
     q_copy.wait()
     dh_copy.wait()
 
@@ -498,10 +471,9 @@
             pltpu.VMEM((2, 1, R), F32),
             pltpu.VMEM((31, 1, R), F32),
             pltpu.VMEM((8, 1, SHARE), F32),
-            dma((6,)), dma((8, 3)), dma((8, 3)), dma((8, 3)), dma((32,)), dma((8,)), dma((8,)), dma((8,)),
-            dma((8,)), dma((8,)), dma((8,)), dma((32,)), dma((8,)), dma((8,)), dma((8,)),
-            dma((8,)), dma((8,)), dma((8, 3)), dma((8, 3)), dma((8,)), dma((8,)),
-            dma((5, 3)), dma((5, 3)), dma((5,)), dma((5,)), dma((31,)), dma((31,)), dma((7,)), dma((7,)),
+            dma((6,)), dma((8, 3)), dma, dma((16,)), dma, dma((8,)), dma, dma((9,)), dma,
+            dma, dma((8,)), dma, dma((8,)), dma, dma((8,)),
+            dma, dma((5,)), dma, dma((5,)), dma, dma, dma, dma,
         ],
         compiler_params=pltpu.CompilerParams(
             collective_id=0, has_side_effects=True, vmem_limit_bytes=62 * 2**20

time: 105 us -> 103 us (0.981)
  Pallas kernels: 101 us -> 98.5 us
    pallas_call x1, Pallas kernels: 101 us -> 98.5 us  [body(): pl.pallas_call(kernel, name='query_path', out_shape=(jax.ShapeDtypeStruct...]
where the time goes in v4:
time: 103 us; the launch traced here: 102 us
  Pallas kernels  98.5 us (96%)
  local copies, waits for them, and re-layouts  3.29 us (3%)
    pallas_call x1, Pallas kernels, body(): pl.pallas_call(kernel, name='query_path', out_shape=(jax.ShapeDtypeStruct...  98.5 us
    unnamed x7, local copies, waits for them, and re-layouts  3.29 us

profile of v4, /device:TPU:1, one launch (start us, length us, event | category | flops | bytes accessed | tf_op | source)
XLA Modules:
  0.0 102.4 jit_solution(6334980223580859724)
XLA Ops:
  0.6 98.5 %query_path.1 = (bf16[256,1536]{1,0:T(8,128)(2,1)}, bf16[320,256]{1,0:T(8,128)(2,1)}, f32[1,96]{1,0:T(1,128)}) custom-call(bf16[320,256]{1,0:T(8,128)(2,1)} %bitcast.4, bf16[48,320]{1,0:T(8,128)(2,1)} %bitcast.6, bf16[48,1536]{1,0:T(8,128)(2,1)} %wu_in.1, f32[1536]{0:T(1024)} %gain_in.1, bf16[256,1536]{1,0:T(8,128)(2,1)} %cot_in.1), custom_call_target="tpu_custom_call" | custom-call | tf_op jit(solution)/shard_map/query_path/pallas_call | solution.py:438
  99.1 0.0 copy-start
  99.1 2.1 %copy.11 = bf16[256,1536]{1,0:T(8,128)(2,1)} copy(bf16[256,1536]{1,0:T(8,128)(2,1)} %get-tuple-element.12) | data formatting | bytes 1572864
  101.2 0.0 copy-done
  101.2 0.0 copy-start.1
  101.2 0.7 copy.12
  101.9 0.0 copy-done.1
  101.9 0.5 copy.13
Async XLA Ops:
  99.1 2.1 %copy-start = (bf16[320,256]{1,0:T(8,128)(2,1)S(1)}, bf16[320,256]{1,0:T(8,128)(2,1)}, u32[]{:S(2)}) copy-start(bf16[320,256]{1,0:T(8,128)(2,1)} %get-tuple-element.7) | copy-start | bytes 491524
  101.2 0.7 copy-start.1

commit v5 on v4

--- a/solution.py
+++ b/solution.py
@@ -27,7 +27,7 @@
     hid_in, wd_in, wu_in, gain_in, cot_in,
     q_out, dh_out, dg_out,
     hid, hid_v, gain_v, gain, cot, qv, dhv,
-    WU, WD, DP, RC, S1, RY, S2, RZ, RES, AGN, AGE, DL, SC, IG, INN, GS, GR, GZ,
+    WU, WD, DP, RC, S1, RY, S2, RZ, RES, AGN, AGE, DL, SC, IG, INN, GS, GP, GR, GZ,
     loc, zr, zs_sem, xr, xs, wzr, wzs, wxr, wxs,
     cs, cr, ys, yr, hs, hr,
     ays, ayr, acs, acr, gs, gr, gzs, gzr,
@@ -259,7 +259,7 @@
         scales = SC[:, 0:1]
         AGE[q, mine] = (scales * (gain[:, q_cols(q)] * dn)).astype(BF16)
         gather1(1 + q, bwd(q))
-        GS[0, :, q_cols(q)] = jnp.sum(dn * RES[q] * scales, axis=0, keepdims=True)
+        GS[:, q_cols(q)] = jnp.sum(dn * RES[q] * scales, axis=0, keepdims=True)
 
     def back5(q):
         gather3(1 + q, bwd(q))
@@ -381,24 +381,21 @@
     fourth()
     chunks(11, 3, 11, back3)
     chunks(12, 3, 11, back3)
+    for k in range(16):
+        GP[k] = GS[:, k * SHARE:(k + 1) * SHARE]
     for n, dev in enumerate(group):
-        send(GS.at[0], GR.at[n], gs, gr, dev)
+        send(GP.at[dev[0]], GR.at[n], gs, gr, dev)
     fifth()
     chunks(12, 4, 12, lambda q: gather2(1 + q, bwd(q)))
     sixth()
     queries(0)
     queries(1)
     chunks(13, 4, 12, lambda q: gather2(1 + q, bwd(q)))
-    total = GS[0]
     arrived(GR, gr)
+    share = GP[lat]
     for n in range(31):
-        total = total + GR[n]
-    GS[1] = total
-    for k in range(16):
-        @pl.when(lat == k)
-        def _():
-            GZ[0] = GS[1, :, k * SHARE:(k + 1) * SHARE]
-
+        share = share + GR[n]
+    GZ[0] = share
     for d in range(1, 8):
         send(GZ.at[0], GZ.at[d], gzs, gzr, zdev((z + d) % 8))
     chunks(13, 5, 13, back5)
@@ -468,8 +465,9 @@
             pltpu.VMEM((32, 128), F32),
             pltpu.VMEM((1, R), F32),
             pltpu.VMEM((TOK, 128), F32),
-            pltpu.VMEM((2, 1, R), F32),
-            pltpu.VMEM((31, 1, R), F32),
+            pltpu.VMEM((1, R), F32),
+            pltpu.VMEM((16, 1, SHARE), F32),
+            pltpu.VMEM((31, 1, SHARE), F32),
             pltpu.VMEM((8, 1, SHARE), F32),
             dma((6,)), dma((8, 3)), dma, dma((16,)), dma, dma((8,)), dma, dma((9,)), dma,
             dma, dma((8,)), dma, dma((8,)), dma, dma((8,)),

time: 103 us -> 101 us (0.981)
  Pallas kernels: 98.5 us -> 97.1 us
    pallas_call x1, Pallas kernels: 98.5 us -> 97.1 us  [body(): pl.pallas_call(kernel, name='query_path', out_shape=(jax.ShapeDtypeStruct...]
where the time goes in v5:
time: 101 us
  Pallas kernels  97.1 us (96%)
  local copies, waits for them, and re-layouts  3.29 us (3%)
    pallas_call x1, Pallas kernels, body(): pl.pallas_call(kernel, name='query_path', out_shape=(jax.ShapeDtypeStruct...  97.1 us
    unnamed x7, local copies, waits for them, and re-layouts  3.29 us

profile of v5, /device:TPU:1, one launch (start us, length us, event | category | flops | bytes accessed | tf_op | source)
XLA Modules:
  0.0 101.1 jit_solution(15788056550810234990)
XLA Ops:
  0.6 97.1 %query_path.1 = (bf16[256,1536]{1,0:T(8,128)(2,1)}, bf16[320,256]{1,0:T(8,128)(2,1)}, f32[1,96]{1,0:T(1,128)}) custom-call(bf16[320,256]{1,0:T(8,128)(2,1)} %bitcast.4, bf16[48,320]{1,0:T(8,128)(2,1)} %bitcast.6, bf16[48,1536]{1,0:T(8,128)(2,1)} %wu_in.1, f32[1536]{0:T(1024)} %gain_in.1, bf16[256,1536]{1,0:T(8,128)(2,1)} %cot_in.1), custom_call_target="tpu_custom_call" | custom-call | tf_op jit(solution)/shard_map/query_path/pallas_call | solution.py:435
  97.8 0.0 copy-start
  97.8 2.1 %copy.11 = bf16[256,1536]{1,0:T(8,128)(2,1)} copy(bf16[256,1536]{1,0:T(8,128)(2,1)} %get-tuple-element.12) | data formatting | bytes 1572864
  99.9 0.0 copy-done
  99.9 0.0 copy-start.1
  99.9 0.7 copy.12
  100.6 0.0 copy-done.1
  100.6 0.5 copy.13
Async XLA Ops:
  97.8 2.1 %copy-start = (bf16[320,256]{1,0:T(8,128)(2,1)S(1)}, bf16[320,256]{1,0:T(8,128)(2,1)}, u32[]{:S(2)}) copy-start(bf16[320,256]{1,0:T(8,128)(2,1)} %get-tuple-element.7) | copy-start | bytes 491524
  99.9 0.7 copy-start.1

commit v6 on v5

--- a/solution.py
+++ b/solution.py
@@ -387,10 +387,8 @@
         send(GP.at[dev[0]], GR.at[n], gs, gr, dev)
     fifth()
     chunks(12, 4, 12, lambda q: gather2(1 + q, bwd(q)))
+    chunks(13, 4, 12, lambda q: gather2(1 + q, bwd(q)))
     sixth()
-    queries(0)
-    queries(1)
-    chunks(13, 4, 12, lambda q: gather2(1 + q, bwd(q)))
     arrived(GR, gr)
     share = GP[lat]
     for n in range(31):
@@ -398,6 +396,8 @@
     GZ[0] = share
     for d in range(1, 8):
         send(GZ.at[0], GZ.at[d], gzs, gzr, zdev((z + d) % 8))
+    queries(0)
+    queries(1)
     chunks(13, 5, 13, back5)
     chunks(14, 5, 13, back5)
     inner = INN[:, 0:1] / R

time: 101 us -> 101 us (level)
  no operation moved by 1% of the time
where the time goes in v6:
time: 101 us
  Pallas kernels  97.1 us (96%)
  local copies, waits for them, and re-layouts  3.29 us (3%)
    pallas_call x1, Pallas kernels, body(): pl.pallas_call(kernel, name='query_path', out_shape=(jax.ShapeDtypeStruct...  97.1 us
    unnamed x7, local copies, waits for them, and re-layouts  3.29 us

profile of v6, /device:TPU:1, one launch (start us, length us, event | category | flops | bytes accessed | tf_op | source)
XLA Modules:
  0.0 101.1 jit_solution(926066255648033087)
XLA Ops:
  0.6 97.1 %query_path.1 = (bf16[256,1536]{1,0:T(8,128)(2,1)}, bf16[320,256]{1,0:T(8,128)(2,1)}, f32[1,96]{1,0:T(1,128)}) custom-call(bf16[320,256]{1,0:T(8,128)(2,1)} %bitcast.4, bf16[48,320]{1,0:T(8,128)(2,1)} %bitcast.6, bf16[48,1536]{1,0:T(8,128)(2,1)} %wu_in.1, f32[1536]{0:T(1024)} %gain_in.1, bf16[256,1536]{1,0:T(8,128)(2,1)} %cot_in.1), custom_call_target="tpu_custom_call" | custom-call | tf_op jit(solution)/shard_map/query_path/pallas_call | solution.py:435
  97.8 0.0 copy-start
  97.8 2.1 %copy.11 = bf16[256,1536]{1,0:T(8,128)(2,1)} copy(bf16[256,1536]{1,0:T(8,128)(2,1)} %get-tuple-element.12) | data formatting | bytes 1572864
  99.9 0.0 copy-done
  99.9 0.0 copy-start.1
  99.9 0.7 copy.12
  100.6 0.0 copy-done.1
  100.6 0.5 copy.13
Async XLA Ops:
  97.8 2.1 %copy-start = (bf16[320,256]{1,0:T(8,128)(2,1)S(1)}, bf16[320,256]{1,0:T(8,128)(2,1)}, u32[]{:S(2)}) copy-start(bf16[320,256]{1,0:T(8,128)(2,1)} %get-tuple-element.7) | copy-start | bytes 491524
  99.9 0.7 copy-start.1
